TPU v7x, 32 devices: a whole 2x2x4 slice. The times are simulated.
32 devices in a mesh: region: 8 (over z, core), layer: 4 (over y, x).
Axes of the slice: x: 2, y: 2, z: 4, core: 2. Of those that a mesh axis runs over, the one named last changes fastest.
Arguments:
- right_side: float32 [64, 131072], P(None, ('region', 'layer')), may hold values from -72 to 72
- block_entries: float32 [2048, 7, 4096], P(('region', 'layer')), may hold values from -0.01875 to 2.01875, as said below
- neighbours: int32 [2048, 6], P(('region', 'layer')), may hold values from 0 to 95
- face_rows: int32 [128, 8], P(('region', 'layer')), may hold values from 0 to 63
- die_owner: int32 [16384, 1], P(('region', 'layer')), may hold values from 0 to 3; in each aligned block of 512 rows (0 to 511, 512 to 1023, ...) at most 128 rows name the same one
- die_node: int32 [16384], P(('region', 'layer')), may hold values from 0 to 4095
Outputs:
- solution_field: float32 [64, 131072], P(None, ('region', 'layer'))
- residual: float32 [64, 131072], P(None, ('region', 'layer'))
- mech_temps: float32 [128, 8192], P(('region', 'layer'))
Inputs may be any that keep to these rules, and one draw needn't show every extreme that they name: `block_entries`: dense blocks of the conduction operator: the diagonal block of each block row carries the node's own coupling on its diagonal. `die_owner`: among the 512 rows of one device, at most 128 name the same owner, and in some devices exactly 128 do.
All inputs are finite; a program needn't handle non-finite values.
Results may differ from a plain program's by a relative error of at most 0.0003.
Values sent between devices are 32-bit elements; how exact they have to be, the bound alone decides.
A program may use at most 128 MiB of HBM per device.

v0:
```python
import jax
import jax.numpy as jnp
from jax import lax
from jax.sharding import PartitionSpec as P

BLOCK = 64
RHS = 64
COUPLED = 7
BLK_DEV = 64
SLOTS = 128
FACES = 8


def partner(shard, axis, bit):
    return lax.ppermute(shard, axis, [(i, i ^ 1 << bit) for i in range(lax.axis_size(axis))])


def with_halo(cells, sides, width):
    for axis, dim in sides:
        count = lax.axis_size(axis)
        ends = count - 1
        head = lax.slice_in_dim(cells, 0, width, axis=dim)
        tail = lax.slice_in_dim(cells, cells.shape[dim] - width, cells.shape[dim], axis=dim)
        cells = jnp.concatenate(
            [
                lax.ppermute(tail, axis, [(i, (i + 1) % count) for i in range(ends)]),
                cells,
                lax.ppermute(head, axis, [((i + 1) % count, i) for i in range(ends)]),
            ],
            axis=dim,
        )
    return cells


def exact_dot(left, right):
    return jnp.dot(left, right, precision=lax.Precision.HIGHEST, preferred_element_type=jnp.float32)


def chol_solve(matrix, target):
    lower_factor = jnp.linalg.cholesky(matrix)
    halfway = lax.linalg.triangular_solve(lower_factor, target, left_side=True, lower=True)
    return lax.linalg.triangular_solve(
        lower_factor, halfway, left_side=True, lower=True, transpose_a=True
    )


def place_rows(values_rows, owners, owner_count):
    owner_hits = (owners[:, None] == jnp.arange(owner_count, dtype=jnp.int32)[None, :]).astype(
        jnp.int32
    )
    earlier_hits = jnp.cumsum(owner_hits, axis=0, dtype=jnp.int32) - owner_hits
    rank_index = jnp.sum(earlier_hits * owner_hits, axis=1, dtype=jnp.int32)
    slot_index = owners * SLOTS + rank_index
    empty_rows = jnp.zeros((owner_count * SLOTS, values_rows.shape[1]), values_rows.dtype)
    return (
        empty_rows.at[slot_index]
        .set(values_rows)
        .reshape(owner_count, SLOTS * values_rows.shape[1])
    )


def on_device(right_side, block_entries, neighbours, face_rows, die_owner, die_node):
    tile_mats = block_entries.reshape(BLK_DEV, COUPLED, BLOCK, BLOCK)
    face_list = face_rows.reshape(-1)
    neighbour_list = neighbours.reshape(-1)
    owners = die_owner[:, 0]
    owner_count = lax.axis_size("layer")
    top_bit = lax.axis_size("region").bit_length() - 2

    def apply_op(field):
        tiles = field.reshape(RHS, BLK_DEV, BLOCK)
        outgoing = jnp.take(tiles, face_list, axis=1).reshape(RHS, 4, FACES * BLOCK)
        near_rows = partner(outgoing[:, 0], "region", 0)
        far_rows = partner(outgoing[:, 1], "region", top_bit)
        stacked = jnp.stack([outgoing[:, 3], outgoing[:, 2]], axis=1)
        layered = with_halo(stacked, (("layer", 1),), 1)
        received = jnp.stack([near_rows, far_rows, layered[:, 0], layered[:, 3]], axis=1)
        extended = jnp.concatenate([tiles, received.reshape(RHS, 4 * FACES, BLOCK)], axis=1)
        picked = jnp.take(extended, neighbour_list, axis=1).reshape(
            RHS, BLK_DEV, COUPLED - 1, BLOCK
        )
        columns = jnp.concatenate([tiles[:, :, None, :], picked], axis=2)
        product = jnp.einsum("snkb,nkab->sna", columns, tile_mats, precision=lax.Precision.HIGHEST)
        return product.reshape(RHS, BLK_DEV * BLOCK)

    norm_zero = lax.psum(exact_dot(right_side, right_side.T), ("region", "layer"))
    image_zero = apply_op(right_side)
    curve_zero = lax.psum(exact_dot(right_side, image_zero.T), ("region", "layer"))
    alpha_first = chol_solve(0.5 * (curve_zero + curve_zero.T), norm_zero)
    iterate_one = exact_dot(alpha_first.T, right_side)
    resid_one = right_side - exact_dot(alpha_first.T, image_zero)
    norm_one = lax.psum(exact_dot(resid_one, resid_one.T), ("region", "layer"))
    beta_step = chol_solve(norm_zero, norm_one)
    direction = resid_one + exact_dot(beta_step.T, right_side)
    image_one = apply_op(direction)
    curve_one = lax.psum(exact_dot(direction, image_one.T), ("region", "layer"))
    alpha_second = chol_solve(0.5 * (curve_one + curve_one.T), norm_one)
    solution_field = iterate_one + exact_dot(alpha_second.T, direction)
    residual = resid_one - exact_dot(alpha_second.T, image_one)
    outgoing_rows = place_rows(jnp.take(solution_field, die_node, axis=1).T, owners, owner_count)
    mech_temps = lax.all_to_all(outgoing_rows, "layer", split_axis=0, concat_axis=0, tiled=True)
    return (solution_field, residual, mech_temps)


def solution(mesh):
    in_specs = (
        P(None, ("region", "layer")),
        P(("region", "layer"), None, None),
        P(("region", "layer"), None),
        P(("region", "layer"), None),
        P(("region", "layer"), None),
        P(("region", "layer")),
    )
    out_specs = (
        P(None, ("region", "layer")),
        P(None, ("region", "layer")),
        P(("region", "layer"), None),
    )
    return jax.shard_map(
        on_device, mesh=mesh, in_specs=in_specs, out_specs=out_specs, check_vma=False
    )
```

profile of v0, /device:TPU:0, one launch (start us, length us, event | category | flops | bytes accessed | tf_op | source)
XLA Modules:
  0.0 364.2 jit_solution(4043952992482037497)
XLA Ops:
  18.7 3.6 collective-permute-start.1
  22.3 4.0 %collective-permute-start.2 = (f32[64,1,512]{2,1,0:T(1,128)}, f32[64,1,512]{2,1,0:T(1,128)}, u32[]{:S(2)}, u32[]{:S(2)}) collective-permute-start(f32[64,1,512]{2,1,0:T(1,128)} %get-tuple-element.15), channel_id=1, source_target_pairs={{0,1},{1,2},{2,3},{4,5},{5,6},{6,7},{8,9},{9,10},{10,11},{12,13},{... | collective-permute-start | bytes 393224 | tf_op jit(solution)/shard_map/ppermute | solution.py:26
  33.4 12.7 %reshape.104 = f32[64,7,64,64]{3,2,0,1:T(8,128)} reshape(f32[64,7,4096]{2,0,1:T(8,128)} %param.16) | data formatting | bytes 14680064 | tf_op jit(solution)/shard_map/reshape | solution.py:63
  46.1 4.1 %copy.80 = f32[64,64,1,64]{3,0,2,1:T(8,128)} copy(f32[64,64,1,64]{3,1,0,2:T(8,128)} %broadcast_in_dim_reshape.6) | data formatting | bytes 2097152 | tf_op jit(solution)/shard_map/broadcast_in_dim;reshape | solution.py:82
  55.8 5.9 %gather_fusion.1 = f32[384,64,64]{2,1,0:T(8,128)} fusion(f32[64,96,64]{2,0,1:T(8,128)S(1)} %pad_maximum_fusion, s32[1024]{0:T(1024)S(1)} %pad_clamp_fusion.1), kind=kCustom, calls=%fused_computation.1.clone | custom fusion | bytes 12584448 | tf_op jit(solution)/shard_map/jit(_take)/gather | solution.py:79
  61.7 10.7 %broadcast_select_fusion.1 = f32[384,64,64]{2,1,0:T(8,128)} fusion(f32[384,64,64]{2,1,0:T(8,128)} %gather_fusion.1, pred[384]{0:T(512)(128)(4,1)S(1)} %compare_and_fusion), kind=kLoop, calls=%fused_computation.17 | loop fusion | flops 1572864 | bytes 12583296 | tf_op jit(solution)/shard_map/jit(_take)/select_n | solution.py:79
  72.4 21.6 %fusion.15 = f32[64,64,64]{2,0,1:T(8,128)S(1)} fusion(f32[64,7,64,64]{3,2,0,1:T(8,128)} %reshape.104, f32[64,64,6,64]{3,0,2,1:T(8,128)} %bitcast.134, f32[64,64,1,64]{3,0,2,1:T(8,128)S(1)} %copy-done.8), kind=kOutput, calls=%fused_computation.25 | convolution fusion | flops 1411121152 | bytes 15728640 | tf_op jit(solution)/shard_map/snkb,nkab->sna/dot_general | solution.py:83
  99.7 42.2 %all-reduce = (f32[64,64]{0,1:T(8,128)S(1)}, f32[64,64]{1,0:T(8,128)S(1)}) all-reduce(f32[64,64]{0,1:T(8,128)S(1)} %fusion.54, f32[64,64]{1,0:T(8,128)S(1)} %convolution_bitcast_fusion), channel_id=1, replica_groups=mesh['region'=8,'layer'=4] {'region','layer'}, use_global_device_ids=true, to_apply=%region_3.7 | all-reduce | flops 8192 | bytes 65536 | tf_op jit(solution)/shard_map/psum | solution.py:86
  142.0 5.8 %cholesky.70 = f32[64,64]{1,0:T(8,128)S(1)} custom-call(f32[64,64]{1,0:T(8,128)S(1)} %fusion.38), custom_call_target="Cholesky" | custom-call | tf_op jit(solution)/shard_map/jit(cholesky)/cholesky | solution.py:40
  149.2 4.9 %custom-call.15 = f32[1,64,64]{1,2,0:T(8,128)S(1)} custom-call(f32[1,64,64]{2,1,0:T(8,128)S(1)} %fusion.26), custom_call_target="InvertDiagBlocksLowerTriangular" | custom-call | tf_op jit(solution)/shard_map/triangular_solve/custom-call.2 | solution.py:42
  154.3 5.8 %cholesky.59 = f32[64,64]{1,0:T(8,128)S(1)} custom-call(f32[64,64]{1,0:T(8,128)S(1)} %fusion.43), custom_call_target="Cholesky" | custom-call | tf_op jit(solution)/shard_map/jit(cholesky)/cholesky | solution.py:40
  161.4 4.9 %custom-call.13 = f32[1,64,64]{1,2,0:T(8,128)S(1)} custom-call(f32[1,64,64]{2,1,0:T(8,128)S(1)} %fusion.25), custom_call_target="InvertDiagBlocksLowerTriangular" | custom-call | tf_op jit(solution)/shard_map/triangular_solve/custom-call.2 | solution.py:42
  168.8 39.8 %psum.30 = f32[64,64]{1,0:T(8,128)S(1)} all-reduce(f32[64,64]{1,0:T(8,128)S(1)} %fusion.56), channel_id=1, replica_groups=mesh['region'=8,'layer'=4] {'region','layer'}, use_global_device_ids=true, to_apply=%region_4.0 | all-reduce | flops 4096 | bytes 32768 | tf_op jit(solution)/shard_map/psum | solution.py:92
  212.2 4.1 %copy.92 = f32[64,64,64]{2,0,1:T(8,128)} copy(f32[64,64,64]{2,1,0:T(8,128)} %reshape.106) | data formatting | bytes 2097152 | tf_op jit(solution)/shard_map/reshape | solution.py:71
  226.8 4.2 %collective-permute-start.6 = (f32[64,1,512]{2,1,0:T(1,128)S(1)}, f32[64,1,512]{2,1,0:T(1,128)S(1)}, u32[]{:S(2)}, u32[]{:S(2)}) collective-permute-start(f32[64,1,512]{2,1,0:T(1,128)S(1)} %get-tuple-element.11), channel_id=1, source_target_pairs={{0,1},{1,2},{2,3},{4,5},{5,6},{6,7},{8,9},{9,10},{10,11},{12,13},{... | collective-permute-start | bytes 393224 | tf_op jit(solution)/shard_map/ppermute | solution.py:26
  236.5 4.1 %copy.94 = f32[64,64,1,64]{3,0,2,1:T(8,128)} copy(f32[64,64,1,64]{3,1,0,2:T(8,128)} %broadcast_in_dim_reshape.7) | data formatting | bytes 2097152 | tf_op jit(solution)/shard_map/broadcast_in_dim;reshape | solution.py:82
  244.3 6.0 %gather_fusion.3 = f32[384,64,64]{2,1,0:T(8,128)} fusion(f32[64,96,64]{2,0,1:T(8,128)S(1)} %pad_maximum_fusion.1, s32[1024]{0:T(1024)S(1)} %pad_clamp_fusion.1), kind=kCustom, calls=%fused_computation.3.clone | custom fusion | bytes 12584448 | tf_op jit(solution)/shard_map/jit(_take)/gather | solution.py:79
  250.4 10.7 %broadcast_select_fusion = f32[384,64,64]{2,1,0:T(8,128)} fusion(f32[384,64,64]{2,1,0:T(8,128)} %gather_fusion.3, pred[384]{0:T(512)(128)(4,1)S(1)} %compare_and_fusion), kind=kLoop, calls=%fused_computation.16 | loop fusion | flops 1572864 | bytes 12583296 | tf_op jit(solution)/shard_map/jit(_take)/select_n | solution.py:79
  261.0 21.5 %fusion.10 = f32[64,64,64]{2,0,1:T(8,128)S(1)} fusion(f32[64,7,64,64]{3,2,0,1:T(8,128)} %reshape.104, f32[64,64,6,64]{3,0,2,1:T(8,128)} %bitcast.133, f32[64,64,1,64]{3,0,2,1:T(8,128)S(1)} %copy-done.7), kind=kOutput, calls=%fused_computation.24 | convolution fusion | flops 1411121152 | bytes 15728640 | tf_op jit(solution)/shard_map/snkb,nkab->sna/dot_general | solution.py:83
  288.3 40.4 %psum.31 = f32[64,64]{1,0:T(8,128)S(1)} all-reduce(f32[64,64]{1,0:T(8,128)S(1)} %fusion.57), channel_id=1, replica_groups=mesh['region'=8,'layer'=4] {'region','layer'}, use_global_device_ids=true, to_apply=%region_5.0 | all-reduce | flops 4096 | bytes 32768 | tf_op jit(solution)/shard_map/psum | solution.py:96
  328.9 5.8 %cholesky.81 = f32[64,64]{1,0:T(8,128)S(1)} custom-call(f32[64,64]{1,0:T(8,128)S(1)} %fusion.32), custom_call_target="Cholesky" | custom-call | tf_op jit(solution)/shard_map/jit(cholesky)/cholesky | solution.py:40
  336.1 4.9 %custom-call.17 = f32[1,64,64]{1,2,0:T(8,128)S(1)} custom-call(f32[1,64,64]{2,1,0:T(8,128)S(1)} %fusion.27), custom_call_target="InvertDiagBlocksLowerTriangular" | custom-call | tf_op jit(solution)/shard_map/triangular_solve/custom-call.2 | solution.py:42
  347.8 4.8 %scatter_custom_fusion = f32[512,64]{1,0:T(8,128)S(1)} fusion(s32[512]{0:T(512)S(1)} %bitcast.143, f32[]{:T(128)} %constant.81.clone.1, f32[]{:T(128)} %constant.75.clone.1, pred[512]{0:T(512)(128)(4,1)S(1)} %compare_and_fusion.2, f32[64,4096]{0,1:T(8,128)} %copy.99, s32[1024]{0:T(1024)S(1)} %pad_clamp_fusion), kind=kCustom, calls=%fused_computation.31 | custom fusion | flops 32768 | bytes 1184264 | tf_op jit(solution)/shard_map/scatter | solution.py:57
  353.4 4.7 %all-to-all-start = ((f32[4,1,8192]{2,1,0:T(1,128)}), f32[4,1,8192]{2,1,0:T(1,128)S(1)}, u32[]{:S(2)}, u32[]{:S(2)}) async-start(f32[4,1,8192]{2,1,0:T(1,128)} %all_to_all.11), calls=%async_computation | async-start | bytes 262144 | tf_op jit(solution)/shard_map/all_to_all | solution.py:101
  (129 shorter events, 85.5 us)
Async XLA Ops:
  4.5 23.6 %copy-start.11 = (s32[64,6]{0,1:T(8,128)S(1)}, s32[64,6]{0,1:T(8,128)}, u32[]{:S(2)}) copy-start(s32[64,6]{0,1:T(8,128)} %param.17) | copy-start | bytes 4612
  4.6 23.9 %copy-start = (f32[64,4096]{1,0:T(8,128)S(1)}, f32[64,4096]{1,0:T(8,128)}, u32[]{:S(2)}) copy-start(f32[64,4096]{1,0:T(8,128)} %param.15) | copy-start | bytes 3145732
  4.6 24.9 %copy-start.10 = (s32[512]{0:T(512)S(1)}, s32[512]{0:T(512)}, u32[]{:S(2)}) copy-start(s32[512]{0:T(512)} %param.20) | copy-start | bytes 6148
  4.6 24.9 %copy-start.9 = (s32[512,1]{0,1:T(1,128)S(1)}, s32[512,1]{0,1:T(1,128)}, u32[]{:S(2)}) copy-start(s32[512,1]{0,1:T(1,128)} %param.19) | copy-start | bytes 6148
  7.5 26.0 %copy-start.6 = (f32[64,64,64]{2,0,1:T(8,128)}, f32[64,64,64]{2,0,1:T(8,128)S(1)}, u32[]{:S(2)}) copy-start(f32[64,64,64]{2,0,1:T(8,128)S(1)} %copy.78) | copy-start | bytes 3145732
  17.5 32.7 %collective-permute-start = (f32[64,512]{1,0:T(8,128)S(1)}, f32[64,512]{1,0:T(8,128)S(1)}, u32[]{:S(2)}, u32[]{:S(2)}) collective-permute-start(f32[64,512]{1,0:T(8,128)S(1)} %bitcast.135), channel_id=1, source_target_pairs={{0,4},{4,0},{8,12},{12,8},{16,20},{20,16},{24,28},{28,24},{1,5},{5... | collective-permute-start | bytes 393224 | tf_op jit(solution)/shard_map/ppermute | solution.py:15
  18.7 31.6 %collective-permute-start.1 = (f32[64,512]{1,0:T(8,128)}, f32[64,512]{1,0:T(8,128)}, u32[]{:S(2)}, u32[]{:S(2)}) collective-permute-start(f32[64,512]{1,0:T(8,128)} %bitcast.129), channel_id=1, source_target_pairs={{0,16},{4,20},{8,24},{12,28},{16,0},{20,4},{24,8},{28,12},{1,17},{... | collective-permute-start | bytes 393224 | tf_op jit(solution)/shard_map/ppermute | solution.py:15
  22.3 29.0 %collective-permute-start.2 = (f32[64,1,512]{2,1,0:T(1,128)}, f32[64,1,512]{2,1,0:T(1,128)}, u32[]{:S(2)}, u32[]{:S(2)}) collective-permute-start(f32[64,1,512]{2,1,0:T(1,128)} %get-tuple-element.15), channel_id=1, source_target_pairs={{0,1},{1,2},{2,3},{4,5},{5,6},{6,7},{8,9},{9,10},{10,11},{12,13},{... | collective-permute-start | bytes 393224 | tf_op jit(solution)/shard_map/ppermute | solution.py:26
  26.4 25.0 %collective-permute-start.3 = (f32[64,1,512]{2,1,0:T(1,128)}, f32[64,1,512]{2,1,0:T(1,128)}, u32[]{:S(2)}, u32[]{:S(2)}) collective-permute-start(f32[64,1,512]{2,1,0:T(1,128)} %get-tuple-element.16), channel_id=1, source_target_pairs={{1,0},{2,1},{3,2},{5,4},{6,5},{7,6},{9,8},{10,9},{11,10},{13,12},{... | collective-permute-start | bytes 393224 | tf_op jit(solution)/shard_map/ppermute | solution.py:28
  61.7 10.7 %copy-start.8 = (f32[64,64,1,64]{3,0,2,1:T(8,128)S(1)}, f32[64,64,1,64]{3,0,2,1:T(8,128)}, u32[]{:S(2)}) copy-start(f32[64,64,1,64]{3,0,2,1:T(8,128)} %copy.80) | copy-start | bytes 3145732
  94.0 4.7 %copy-start.1 = (f32[64,4096]{1,0:T(8,128)S(1)}, f32[64,4096]{1,0:T(8,128)}, u32[]{:S(2)}) copy-start(f32[64,4096]{1,0:T(8,128)} %param.15) | copy-start | bytes 3145732
  167.8 51.7 %copy-start.4 = (f32[64,4096]{1,0:T(8,128)}, f32[64,4096]{1,0:T(8,128)S(1)}, u32[]{:S(2)}) copy-start(f32[64,4096]{1,0:T(8,128)S(1)} %convolution_subtract_fusion.1) | copy-start | bytes 3145732
  210.0 24.3 %copy-start.2 = (f32[64,4096]{1,0:T(8,128)}, f32[64,4096]{1,0:T(8,128)S(1)}, u32[]{:S(2)}) copy-start(f32[64,4096]{1,0:T(8,128)S(1)} %convolution_add_fusion.1) | copy-start | bytes 3145732
  225.0 15.6 %collective-permute-start.4 = (f32[64,512]{1,0:T(8,128)S(1)}, f32[64,512]{1,0:T(8,128)S(1)}, u32[]{:S(2)}, u32[]{:S(2)}) collective-permute-start(f32[64,512]{1,0:T(8,128)S(1)} %bitcast.136), channel_id=1, source_target_pairs={{0,4},{4,0},{8,12},{12,8},{16,20},{20,16},{24,28},{28,24},{1,5},{5... | collective-permute-start | bytes 393224 | tf_op jit(solution)/shard_map/ppermute | solution.py:15
  225.1 15.6 %collective-permute-start.5 = (f32[64,512]{1,0:T(8,128)S(1)}, f32[64,512]{1,0:T(8,128)S(1)}, u32[]{:S(2)}, u32[]{:S(2)}) collective-permute-start(f32[64,512]{1,0:T(8,128)S(1)} %bitcast.137), channel_id=1, source_target_pairs={{0,16},{4,20},{8,24},{12,28},{16,0},{20,4},{24,8},{28,12},{1,17},{... | collective-permute-start | bytes 393224 | tf_op jit(solution)/shard_map/ppermute | solution.py:15
  226.8 14.0 %collective-permute-start.6 = (f32[64,1,512]{2,1,0:T(1,128)S(1)}, f32[64,1,512]{2,1,0:T(1,128)S(1)}, u32[]{:S(2)}, u32[]{:S(2)}) collective-permute-start(f32[64,1,512]{2,1,0:T(1,128)S(1)} %get-tuple-element.11), channel_id=1, source_target_pairs={{0,1},{1,2},{2,3},{4,5},{5,6},{6,7},{8,9},{9,10},{10,11},{12,13},{... | collective-permute-start | bytes 393224 | tf_op jit(solution)/shard_map/ppermute | solution.py:26
  231.0 9.8 %collective-permute-start.7 = (f32[64,1,512]{2,1,0:T(1,128)S(1)}, f32[64,1,512]{2,1,0:T(1,128)S(1)}, u32[]{:S(2)}, u32[]{:S(2)}) collective-permute-start(f32[64,1,512]{2,1,0:T(1,128)S(1)} %get-tuple-element.12), channel_id=1, source_target_pairs={{1,0},{2,1},{3,2},{5,4},{6,5},{7,6},{9,8},{10,9},{11,10},{13,12},{... | collective-permute-start | bytes 393224 | tf_op jit(solution)/shard_map/ppermute | solution.py:28
  250.4 10.7 %copy-start.7 = (f32[64,64,1,64]{3,0,2,1:T(8,128)S(1)}, f32[64,64,1,64]{3,0,2,1:T(8,128)}, u32[]{:S(2)}) copy-start(f32[64,64,1,64]{3,0,2,1:T(8,128)} %copy.94) | copy-start | bytes 3145732
  282.5 4.8 %copy-start.3 = (f32[64,4096]{1,0:T(8,128)S(1)}, f32[64,4096]{1,0:T(8,128)}, u32[]{:S(2)}) copy-start(f32[64,4096]{1,0:T(8,128)} %copy-done.2) | copy-start | bytes 3145732
  285.1 73.1 %copy-start.5 = (f32[64,4096]{1,0:T(8,128)S(1)}, f32[64,4096]{1,0:T(8,128)}, u32[]{:S(2)}) copy-start(f32[64,4096]{1,0:T(8,128)} %copy-done.4) | copy-start | bytes 3145732
  353.4 9.7 %all-to-all-start = ((f32[4,1,8192]{2,1,0:T(1,128)}), f32[4,1,8192]{2,1,0:T(1,128)S(1)}, u32[]{:S(2)}, u32[]{:S(2)}) async-start(f32[4,1,8192]{2,1,0:T(1,128)} %all_to_all.11), calls=%async_computation | async-start | bytes 262144 | tf_op jit(solution)/shard_map/all_to_all | solution.py:101
where the time goes:
time: 369 us; the launch traced here: 364 us
  blocking collectives  122 us (33%)
  local copies, waits for them, and re-layouts  85.2 us (23%)
  other arithmetic  72.6 us (20%)
  matrix products  57.6 us (16%)
  starting transfers between devices  22 us (6%)
    dot_general x2, matrix products, apply_op(): jnp.einsum('snkb,nkab->sna', columns, tile_mats, precision=lax.Precision....  43.1 us
    psum x1, blocking collectives, on_device(): lax.psum(exact_dot(right_side, right_side.T), ('region', 'layer'))  42.2 us
    psum x1, blocking collectives, on_device(): curve_one = lax.psum(exact_dot(direction, image_one.T), ('region', 'layer'))  40.4 us
    psum x1, blocking collectives, on_device(): norm_one = lax.psum(exact_dot(resid_one, resid_one.T), ('region', 'layer'))  39.8 us
    select_n x3, other arithmetic, apply_op(): jnp.take(extended, neighbour_list, axis=1)  21.3 us
    another operation x9, other arithmetic, chol_solve(): lower_factor = jnp.linalg.cholesky(matrix)  19.6 us
    another operation x6, other arithmetic, chol_solve(): lax.linalg.triangular_solve(lower_factor, halfway, left_side=True, lower=...  16.6 us
    dot_general x9, matrix products, exact_dot(): jnp.dot(left, right, precision=lax.Precision.HIGHEST, preferred_element_t...  13.2 us
  transfers between devices with their start and end apart: 9, of which 1 were waited for; matrix products, arithmetic and copies ran while one was open for 9% of the time, Pallas kernels for 0%

commit v1 on v0

v1 whole, which is shorter than its diff:
```python
import functools

import jax
import jax.numpy as jnp
from jax import lax
from jax.experimental import pallas as pl
from jax.experimental.pallas import tpu as pltpu
from jax.sharding import PartitionSpec as P

BLOCK = 64
RHS = 64
COUPLED = 7
BLK_DEV = 64
SLOTS = 128
FACES = 8
GROUP = 8
MESH = pl.DeviceIdType.MESH
F32 = jnp.float32
BF16 = jnp.bfloat16
VMEM = functools.partial(pl.BlockSpec, memory_space=pltpu.VMEM)
SMEM = functools.partial(pl.BlockSpec, memory_space=pltpu.SMEM)
BIG = 48 * 1024 * 1024


def dot_hi(left, right, dims=((1,), (0,))):
    return lax.dot_general(
        left, right, (dims, ((), ())), precision=lax.Precision.HIGHEST, preferred_element_type=F32
    )


def exchange_kernel(regions, layers, faces_ref, field_ref, out_ref, send_buf, send_sem, recv_sem):
    region = lax.axis_index("region")
    layer = lax.axis_index("layer")
    near = region + 1 - 2 * lax.rem(region, 2)
    far = lax.rem(region + regions // 2, regions)
    peers = (
        (near, layer),
        (far, layer),
        (region, lax.max(layer - 1, 0)),
        (region, lax.min(layer + 1, layers - 1)),
    )
    has = (None, None, layer > 0, layer < layers - 1)
    landing = (0, 1, 3, 2)

    def guarded(m, action):
        if has[m] is None:
            action()
        else:
            pl.when(has[m])(action)

    barrier = pltpu.get_barrier_semaphore()
    for m in range(4):

        def greet(m=m):
            pl.semaphore_signal(barrier, inc=1, device_id=peers[m], device_id_type=MESH)

        guarded(m, greet)
    for m in range(4):
        for j in range(FACES // 2):
            first = field_ref[faces_ref[m * FACES + 2 * j]]
            second = field_ref[faces_ref[m * FACES + 2 * j + 1]]
            send_buf[m, j] = jnp.concatenate([first, second], axis=1)
    pl.semaphore_wait(barrier, 2 + lax.min(layer, 1) + lax.min(layers - 1 - layer, 1))

    def copy_of(m):
        return pltpu.make_async_remote_copy(
            src_ref=send_buf.at[SENDS[m]],
            dst_ref=out_ref.at[landing[m]],
            send_sem=send_sem.at[m],
            recv_sem=recv_sem.at[landing[m]],
            device_id=peers[m],
            device_id_type=MESH,
        )

    for m in range(4):
        guarded(m, lambda m=m: copy_of(m).start())
    for m in (2, 3):

        def blank(m=m):
            out_ref[m] = jnp.zeros_like(out_ref[m])

        pl.when(jnp.logical_not(has[m]))(blank)
    for m in range(4):
        guarded(m, lambda m=m: copy_of(m).wait_send())
    for m in range(4):

        def arrive(m=m):
            pltpu.make_async_remote_copy(
                src_ref=send_buf.at[m],
                dst_ref=out_ref.at[m],
                send_sem=send_sem.at[m],
                recv_sem=recv_sem.at[m],
                device_id=peers[m],
                device_id_type=MESH,
            ).wait_recv()

        guarded(m, arrive)


SENDS = (0, 1, 3, 2)


def exchange(faces, field, regions, layers, number):
    return pl.pallas_call(
        functools.partial(exchange_kernel, regions, layers),
        out_shape=jax.ShapeDtypeStruct((4, FACES // 2, BLOCK, 2 * RHS), F32),
        in_specs=[SMEM(), VMEM()],
        out_specs=VMEM(),
        scratch_shapes=[
            pltpu.VMEM((4, FACES // 2, BLOCK, 2 * RHS), F32),
            pltpu.SemaphoreType.DMA((4,)),
            pltpu.SemaphoreType.DMA((4,)),
        ],
        compiler_params=pltpu.CompilerParams(
            collective_id=number, has_side_effects=True, vmem_limit_bytes=BIG
        ),
        name="face_exchange",
    )(faces, field)


def split_pair(block):
    upper = block.astype(BF16)
    return upper, (block - upper.astype(F32)).astype(BF16)


def load_extended(field_ref, recv_ref, ext):
    @pl.loop(0, BLK_DEV, unroll=4)
    def _(n):
        upper, lower = split_pair(field_ref[n])
        ext[n] = jnp.concatenate([upper, lower], axis=1)

    for m in range(4):
        for j in range(FACES // 2):
            pair = recv_ref[m, j]
            for half in range(2):
                upper, lower = split_pair(pair[:, half * RHS : (half + 1) * RHS])
                ext[BLK_DEV + m * FACES + 2 * j + half] = jnp.concatenate([upper, lower], axis=1)


def product_of(left, neigh_ref, ext, i):
    parts = [ext[i]]
    for k in range(COUPLED - 1):
        parts.append(ext[neigh_ref[i * (COUPLED - 1) + k]])
    full = jnp.dot(left, jnp.concatenate(parts, axis=0), preferred_element_type=F32)
    rows = full[:BLOCK] + full[BLOCK:]
    return rows[:, :RHS] + rows[:, RHS:]


def first_kernel(neigh_ref, mats_ref, field_ref, recv_ref, out_ref, left_ref, ext, spread):
    group = pl.program_id(0)

    @pl.when(group == 0)
    def _():
        load_extended(field_ref, recv_ref, ext)

    for k in range(COUPLED):
        for c in range(BLOCK // 2):
            spread[k, pl.ds(c * GROUP, GROUP), :] = mats_ref[k, :, c * 128 : (c + 1) * 128]
    low = lax.broadcasted_iota(jnp.int32, (BLOCK // 2, 128), 1) < BLOCK
    for sub in range(GROUP):
        i = group * GROUP + sub
        tiles = [spread[k, pl.ds(sub, BLOCK // 2, stride=GROUP), :] for k in range(COUPLED)]
        turned = [pltpu.roll(tile, BLOCK, 1) for tile in tiles]
        uppers, lowers = [], []
        for k in range(0, COUPLED, 2):
            if k + 1 < COUPLED:
                even = jnp.where(low, tiles[k], turned[k + 1])
                odd = jnp.where(low, turned[k], tiles[k + 1])
            else:
                even, odd = tiles[k][:, :BLOCK], turned[k][:, :BLOCK]
            upper, lower = split_pair(jnp.concatenate([even, odd], axis=0))
            uppers.append(upper)
            lowers.append(lower)
        left = jnp.concatenate(
            [jnp.concatenate(uppers, axis=1), jnp.concatenate(lowers, axis=1)], axis=0
        )
        left_ref[sub] = left
        rows = product_of(left, neigh_ref, ext, i)
        for odd in range(2):
            out_ref[pl.ds(sub * BLOCK + odd, BLOCK // 2, stride=2), :] = rows[
                odd * BLOCK // 2 : (odd + 1) * BLOCK // 2
            ]


def second_kernel(neigh_ref, left_ref, field_ref, recv_ref, base_ref, near_ref, out_ref, gram_ref, ext):
    group = pl.program_id(0)

    @pl.when(group == 0)
    def _():
        load_extended(field_ref, recv_ref, ext)
        gram_ref[...] = jnp.zeros_like(gram_ref)

    for sub in range(GROUP):
        i = group * GROUP + sub
        rows = product_of(left_ref[sub], neigh_ref, ext, i)
        for odd in range(2):
            out_ref[pl.ds(sub * BLOCK + odd, BLOCK // 2, stride=2), :] = rows[
                odd * BLOCK // 2 : (odd + 1) * BLOCK // 2
            ]
    pair = jnp.concatenate([base_ref[...], near_ref[...]], axis=1)
    own = dot_hi(pair, pair, ((0,), (0,)))
    cross = dot_hi(pair, out_ref[...], ((0,), (0,)))
    gram_ref[0:64] += own[:64]
    gram_ref[64:128] += jnp.concatenate([own[64:, 64:], cross[:64]], axis=1)
    gram_ref[128:192] += jnp.concatenate([cross[64:], cross[64:]], axis=1)


def apply_first(neigh, mats, field, recv):
    rows = GROUP * BLOCK
    grid = BLK_DEV // GROUP
    return pl.pallas_call(
        first_kernel,
        grid=(grid,),
        out_shape=[
            jax.ShapeDtypeStruct((BLK_DEV * BLOCK, RHS), F32),
            jax.ShapeDtypeStruct((BLK_DEV, 2 * BLOCK, COUPLED * BLOCK), BF16),
        ],
        in_specs=[
            SMEM(),
            pl.BlockSpec((COUPLED, GROUP, BLOCK * BLOCK), lambda g: (0, g, 0)),
            pl.BlockSpec((BLK_DEV, BLOCK, RHS), lambda g: (0, 0, 0)),
            pl.BlockSpec((4, FACES // 2, BLOCK, 2 * RHS), lambda g: (0, 0, 0, 0)),
        ],
        out_specs=[
            pl.BlockSpec((rows, RHS), lambda g: (g, 0)),
            pl.BlockSpec((GROUP, 2 * BLOCK, COUPLED * BLOCK), lambda g: (g, 0, 0)),
        ],
        scratch_shapes=[
            pltpu.VMEM((BLK_DEV + 4 * FACES, BLOCK, 2 * RHS), BF16),
            pltpu.VMEM((COUPLED, GROUP * BLOCK // 2, 128), F32),
        ],
        compiler_params=pltpu.CompilerParams(vmem_limit_bytes=BIG),
        name="operator_first",
    )(neigh, mats, field, recv)


def apply_second(neigh, lefts, field, recv, base):
    rows = GROUP * BLOCK
    grid = BLK_DEV // GROUP
    return pl.pallas_call(
        second_kernel,
        grid=(grid,),
        out_shape=[
            jax.ShapeDtypeStruct((BLK_DEV * BLOCK, RHS), F32),
            jax.ShapeDtypeStruct((192, 128), F32),
        ],
        in_specs=[
            SMEM(),
            pl.BlockSpec((GROUP, 2 * BLOCK, COUPLED * BLOCK), lambda g: (g, 0, 0)),
            pl.BlockSpec((BLK_DEV, BLOCK, RHS), lambda g: (0, 0, 0)),
            pl.BlockSpec((4, FACES // 2, BLOCK, 2 * RHS), lambda g: (0, 0, 0, 0)),
            pl.BlockSpec((rows, RHS), lambda g: (g, 0)),
            pl.BlockSpec((rows, RHS), lambda g: (g, 0)),
        ],
        out_specs=[
            pl.BlockSpec((rows, RHS), lambda g: (g, 0)),
            pl.BlockSpec((192, 128), lambda g: (0, 0)),
        ],
        scratch_shapes=[pltpu.VMEM((BLK_DEV + 4 * FACES, BLOCK, 2 * RHS), BF16)],
        compiler_params=pltpu.CompilerParams(vmem_limit_bytes=BIG),
        name="operator_second",
    )(neigh, lefts, field.reshape(BLK_DEV, BLOCK, RHS), recv, base, field)


def sum_kernel(regions, layers, part_ref, out_ref, hold_core, total, hold_layer, hold_chip, sems):
    region = lax.axis_index("region")
    layer = lax.axis_index("layer")
    chips = regions // 2
    core = lax.rem(region, 2)
    chip = lax.div(region, 2)
    others = (
        [(2 * chip + 1 - core, layer)]
        + [(region, lax.rem(layer + d, layers)) for d in range(1, layers)]
        + [(2 * lax.rem(chip + d, chips) + core, layer) for d in range(1, chips)]
    )
    barrier = pltpu.get_barrier_semaphore()
    for peer in others:
        pl.semaphore_signal(barrier, inc=1, device_id=peer, device_id_type=MESH)
    pl.semaphore_wait(barrier, len(others))

    def copy_of(n, source, target):
        return pltpu.make_async_remote_copy(
            src_ref=source,
            dst_ref=target,
            send_sem=sems.at[0, n],
            recv_sem=sems.at[1, n],
            device_id=others[n],
            device_id_type=MESH,
        )

    copies = [copy_of(0, part_ref, hold_core)]
    copies[0].start()
    copies[0].wait_recv()
    total[0] = part_ref[...] + hold_core[...]
    stage = [copy_of(d, total.at[0], hold_layer.at[d - 1]) for d in range(1, layers)]
    for copy in stage:
        copy.start()
    for copy in stage:
        copy.wait_recv()
    value = total[0]
    for d in range(layers - 1):
        value = value + hold_layer[d]
    total[1] = value
    copies += stage
    stage = [copy_of(layers - 1 + d, total.at[1], hold_chip.at[d - 1]) for d in range(1, chips)]
    for copy in stage:
        copy.start()
    for copy in stage:
        copy.wait_recv()
    for d in range(chips - 1):
        value = value + hold_chip[d]
    out_ref[...] = value
    copies += stage
    for copy in copies:
        copy.wait_send()


def sum_all(part, regions, layers, number):
    shape = part.shape
    chips = regions // 2
    return pl.pallas_call(
        functools.partial(sum_kernel, regions, layers),
        out_shape=jax.ShapeDtypeStruct(shape, F32),
        in_specs=[VMEM()],
        out_specs=VMEM(),
        scratch_shapes=[
            pltpu.VMEM(shape, F32),
            pltpu.VMEM((2,) + shape, F32),
            pltpu.VMEM((layers - 1,) + shape, F32),
            pltpu.VMEM((chips - 1,) + shape, F32),
            pltpu.SemaphoreType.DMA((2, layers + chips - 1)),
        ],
        compiler_params=pltpu.CompilerParams(
            collective_id=number, has_side_effects=True, vmem_limit_bytes=BIG
        ),
        name="gram_sum",
    )(part)


def eliminate(works):
    row_id = lax.broadcasted_iota(jnp.int32, (RHS, 2 * RHS), 0)
    for k in range(RHS):
        done = []
        for work in works:
            scaled = work[k : k + 1, :] * (1.0 / work[k : k + 1, k : k + 1])
            done.append(jnp.where(row_id == k, scaled, work - work[:, k : k + 1] * scaled))
        works = done
    return [work[:, RHS:] for work in works]


def solve_kernel(gram_ref, out_ref):
    norm_zero = gram_ref[0:64, 0:64]
    curve_zero = gram_ref[0:64, 64:128]
    image_gram = gram_ref[64:128, 0:64]
    base_twice = gram_ref[64:128, 64:128]
    image_twice = gram_ref[128:192, 0:64]
    eye = (
        lax.broadcasted_iota(jnp.int32, (RHS, RHS), 0)
        == lax.broadcasted_iota(jnp.int32, (RHS, RHS), 1)
    ).astype(F32)
    symmetric = 0.5 * (curve_zero + curve_zero.T)
    alpha, inverse = eliminate(
        [
            jnp.concatenate([symmetric, norm_zero], axis=1),
            jnp.concatenate([norm_zero, eye], axis=1),
        ]
    )
    crossed = dot_hi(curve_zero, alpha)
    norm_one = norm_zero - crossed - crossed.T + dot_hi(alpha, dot_hi(image_gram, alpha), ((0,), (0,)))
    blend = eye + dot_hi(inverse, norm_one)
    upper = dot_hi(curve_zero, blend) - dot_hi(base_twice, alpha)
    lower = dot_hi(image_gram, blend) - dot_hi(image_twice, alpha)
    curve_one = dot_hi(blend, upper, ((0,), (0,))) - dot_hi(alpha, lower, ((0,), (0,)))
    (alpha_second,) = eliminate(
        [jnp.concatenate([0.5 * (curve_one + curve_one.T), norm_one], axis=1)]
    )
    out_ref[0:64] = alpha + dot_hi(blend, alpha_second)
    out_ref[64:128] = -dot_hi(alpha, alpha_second)


def solve_all(gram):
    return pl.pallas_call(
        solve_kernel,
        out_shape=jax.ShapeDtypeStruct((2 * RHS, RHS), F32),
        in_specs=[VMEM()],
        out_specs=VMEM(),
        name="small_solves",
    )(gram)


def final_kernel(mix_ref, base_ref, image_ref, twice_ref, sol_ref, res_ref):
    first = mix_ref[0:64]
    second = mix_ref[64:128]
    over = ((0,), (1,))
    base = base_ref[...]
    image = image_ref[...]
    sol_ref[...] = dot_hi(first, base, ((0,), (0,))) + dot_hi(second, image, over)
    res_ref[...] = base - (dot_hi(first, image, over) + dot_hi(second, twice_ref[...], over))


def final_fields(mix, base, image, twice):
    nodes = base.shape[1]
    step = nodes // 4
    wide = pl.BlockSpec((RHS, step), lambda g: (0, g))
    tall = pl.BlockSpec((step, RHS), lambda g: (g, 0))
    return pl.pallas_call(
        final_kernel,
        grid=(nodes // step,),
        out_shape=[jax.ShapeDtypeStruct(base.shape, F32)] * 2,
        in_specs=[pl.BlockSpec((2 * RHS, RHS), lambda g: (0, 0)), wide, tall, tall],
        out_specs=[wide, wide],
        compiler_params=pltpu.CompilerParams(vmem_limit_bytes=BIG),
        name="final_fields",
    )(mix, base, image, twice)


def place_kernel(slot_ref, node_ref, base_ref, image_ref, out_ref):
    out_ref[...] = jnp.zeros_like(out_ref)

    @pl.loop(0, slot_ref.shape[0], unroll=8)
    def _(j):
        slot, node = slot_ref[j], node_ref[j]
        row = jnp.concatenate([base_ref[pl.ds(node, 1), :], image_ref[pl.ds(node, 1), :]], axis=1)
        out_ref[pl.ds(slot, 1), :] = row


def place_rows(slots, nodes, base, image, count):
    return pl.pallas_call(
        place_kernel,
        out_shape=jax.ShapeDtypeStruct((count * SLOTS, 2 * RHS), F32),
        in_specs=[SMEM(), SMEM(), VMEM(), VMEM()],
        out_specs=VMEM(),
        compiler_params=pltpu.CompilerParams(vmem_limit_bytes=BIG),
        name="place_rows",
    )(slots, nodes, base, image)


def slots_of(owners, owner_count):
    hits = (owners[:, None] == jnp.arange(owner_count, dtype=jnp.int32)[None, :]).astype(jnp.int32)
    earlier = jnp.cumsum(hits, axis=0, dtype=jnp.int32) - hits
    return owners * SLOTS + jnp.sum(earlier * hits, axis=1, dtype=jnp.int32)


def on_device(right_side, block_entries, neighbours, face_rows, die_owner, die_node):
    regions, layers = lax.axis_size("region"), lax.axis_size("layer")
    mats = block_entries.transpose(1, 0, 2)
    faces = face_rows.reshape(-1)
    neigh = neighbours.reshape(-1)
    base = right_side.T
    base_blocks = base.reshape(BLK_DEV, BLOCK, RHS)
    slots = slots_of(die_owner[:, 0], layers)
    received = exchange(faces, base_blocks, regions, layers, 0)
    image, lefts = apply_first(neigh, mats, base_blocks, received)
    received = exchange(faces, image.reshape(BLK_DEV, BLOCK, RHS), regions, layers, 0)
    twice, gram = apply_second(neigh, lefts, image, received, base)
    placed = place_rows(slots, die_node, base, image, layers)
    arrived = lax.all_to_all(
        placed.reshape(layers, SLOTS, 2 * RHS), "layer", split_axis=0, concat_axis=0, tiled=True
    )
    mix = solve_all(sum_all(gram, regions, layers, 1))
    solution_field, residual = final_fields(mix, right_side, image, twice)
    mech = jnp.dot(
        arrived.reshape(layers * SLOTS, 2 * RHS),
        mix,
        precision=lax.Precision.HIGHEST,
        preferred_element_type=F32,
    )
    return solution_field, residual, mech.reshape(layers, SLOTS * RHS)


def solution(mesh):
    in_specs = (
        P(None, ("region", "layer")),
        P(("region", "layer"), None, None),
        P(("region", "layer"), None),
        P(("region", "layer"), None),
        P(("region", "layer"), None),
        P(("region", "layer")),
    )
    out_specs = (
        P(None, ("region", "layer")),
        P(None, ("region", "layer")),
        P(("region", "layer"), None),
    )
    return jax.shard_map(
        on_device, mesh=mesh, in_specs=in_specs, out_specs=out_specs, check_vma=False
    )
```

time: 369 us -> 109 us (0.30); the launches traced: 364 us -> 108 us
  blocking collectives: 122 us -> 0 us
  Pallas kernels: 0 us -> 93 us
  local copies, waits for them, and re-layouts: 85.2 us -> 9.2 us
  other arithmetic: 72.6 us -> 1.52 us
  matrix products: 57.6 us -> 0.36 us
  starting transfers between devices: 22 us -> 3.4 us
    psum x3 -> x0, blocking collectives: 122 us -> none  [the longest x1 42.2 us: on_device(): lax.psum(exact_dot(right_side, right_side.T), ('region', 'layer'))]
    pallas_call x0 -> x8, Pallas kernels: none -> 93 us  [the longest x2 21.5 us: exchange(): pl.pallas_call(functools.partial(exchange_kernel, regions, layers), out_s...]
    dot_general x11 -> x1, matrix products: 56.3 us -> 0.36 us  [on_device(): jnp.dot(arrived.reshape(layers * SLOTS, 2 * RHS), mix, precision=lax.Prec...]
    another operation x19 -> x2, other arithmetic: 39.6 us -> 1.41 us  [the longest x9 19.6 us: chol_solve(): lower_factor = jnp.linalg.cholesky(matrix)]
    reshape x15 -> x3, local copies, waits for them, and re-layouts: 35.7 us -> 1.01 us  [the longest x1 0.79 us: on_device(): return (solution_field, residual, mech.reshape(layers, SLOTS * RHS))]
    select_n x8 -> x0, other arithmetic: 24.1 us -> none  [the longest x3 21.3 us: apply_op(): jnp.take(extended, neighbour_list, axis=1)]
    ppermute x8 -> x0, starting transfers between devices: 17.2 us -> none  [the longest x2 8.2 us: with_halo(): lax.ppermute(tail, axis, [(i, (i + 1) % count) for i in range(ends)])]
    gather x4 -> x0, local copies, waits for them, and re-layouts: 16.7 us -> none  [the longest x2 11.9 us: apply_op(): jnp.take(extended, neighbour_list, axis=1)]
  transfers between devices with their start and end apart: 9 -> 1, of which waited for: 1 -> 0; matrix products, arithmetic and copies ran while one was open for 9% -> 0% of each run, Pallas kernels for 0% -> 59%
where the time goes in v1:
time: 109 us; the launch traced here: 108 us
  Pallas kernels  93 us (85%)
  local copies, waits for them, and re-layouts  9.2 us (8%)
  starting transfers between devices  3.4 us (3%)
  other arithmetic  1.52 us (1%)
    pallas_call x2, Pallas kernels, exchange(): pl.pallas_call(functools.partial(exchange_kernel, regions, layers), out_s...  21.5 us
    pallas_call x1, Pallas kernels, sum_all(): pl.pallas_call(functools.partial(sum_kernel, regions, layers), out_shape=...  18.6 us
    pallas_call x1, Pallas kernels, solve_all(): pl.pallas_call(solve_kernel, out_shape=jax.ShapeDtypeStruct((2 * RHS, RHS...  14.4 us
    pallas_call x1, Pallas kernels, apply_second(): pl.pallas_call(second_kernel, grid=(grid,), out_shape=[jax.ShapeDtypeStru...  12 us
    pallas_call x1, Pallas kernels, apply_first(): pl.pallas_call(first_kernel, grid=(grid,), out_shape=[jax.ShapeDtypeStruc...  11.2 us
    pallas_call x1, Pallas kernels, final_fields(): pl.pallas_call(final_kernel, grid=(nodes // step,), out_shape=[jax.ShapeD...  8.97 us
    unnamed x30, local copies, waits for them, and re-layouts  7.97 us
    pallas_call x1, Pallas kernels, place_rows(): pl.pallas_call(place_kernel, out_shape=jax.ShapeDtypeStruct((count * SLOT...  6.21 us
  transfers between devices with their start and end apart: 1, of which 0 were waited for; matrix products, arithmetic and copies ran while one was open for 0% of the time, Pallas kernels for 59%

profile of v1, /device:TPU:0, one launch (start us, length us, event | category | flops | bytes accessed | tf_op | source)
XLA Modules:
  0.0 108.3 jit_solution(11099806822151893027)
XLA Ops:
  0.7 1.8 %copy.11 = f32[64,4096]{0,1:T(8,128)S(1)} copy(f32[64,4096]{1,0:T(8,128)} %base_ref.1) | data formatting | bytes 2097152 | tf_op args[0]
  2.5 0.1 reshape.46.faces_ref
  2.6 0.1 copy.10
  2.7 0.1 reshape.44.neigh_ref
  2.9 1.2 %reduce-window.6 = s32[4,4,128]{2,1,0:T(4,128)S(1)} reduce-window(s32[4,4,128]{2,1,0:T(4,128)S(1)} %fusion.3, s32[]{:T(128)} %constant.7.clone.1), window={size=1x1x128 pad=0_0x0_0x127_0}, to_apply=%region_0.0 | reduce-window | flops 260096 | bytes 16388 | tf_op jit(solution)/shard_map/reduce-window
  4.1 0.2 slice_reduce_fusion
  4.3 0.2 reduce-window.9
  4.5 0.1 add_bitcast_fusion
  4.6 12.2 %face_exchange.2.recv_ref = f32[4,4,64,128]{3,2,1,0:T(8,128)S(1)} custom-call(s32[32]{0:T(128)S(1)} %reshape.46.faces_ref, f32[64,64,64]{2,1,0:T(8,128)S(1)} %bitcast.30), custom_call_target="tpu_custom_call" | custom-call | tf_op jit(solution)/shard_map/face_exchange/pallas_call | solution.py:104
  16.8 11.2 %operator_first.1 = (f32[4096,64]{1,0:T(8,128)S(1)}, bf16[64,128,448]{2,1,0:T(8,128)(2,1)}) custom-call(s32[384]{0:T(512)S(1)} %reshape.44.neigh_ref, f32[7,64,4096]{2,1,0:T(8,128)} %bitcast.36, f32[64,64,64]{2,1,0:T(8,128)S(1)} %bitcast.31, f32[4,4,64,128]{3,2,1,0:T(8,128)S(1)} %face_exchange.2.recv_ref), custom_call_target="tpu_custom_call" | custom-call | tf_op jit(solution)/shard_map/operator_first/pallas_call | solution.py:211
  28.0 6.2 %place_rows.1 = f32[512,128]{1,0:T(8,128)} custom-call(s32[512]{0:T(512)S(1)} %multiply_add_fusion.slot_ref, s32[512]{0:T(512)S(1)} %copy-done.10, f32[4096,64]{1,0:T(8,128)S(1)} %bitcast.32, f32[4096,64]{1,0:T(8,128)S(1)} %get-tuple-element.10.near_ref.image_ref), custom_call_target="tpu_custom_call" | custom-call | tf_op jit(solution)/shard_map/place_rows/pallas_call | solution.py:428
  34.2 3.4 %all-to-all-start = ((f32[4,128,128]{2,1,0:T(8,128)}), f32[4,128,128]{2,1,0:T(8,128)S(1)}, u32[]{:S(2)}, u32[]{:S(2)}) async-start(f32[4,128,128]{2,1,0:T(8,128)} %bitcast.8), calls=%async_computation | async-start | bytes 524288 | tf_op jit(solution)/shard_map/all_to_all | solution.py:457
  37.6 1.6 %copy-done.2 = f32[4096,64]{1,0:T(8,128)S(1)} copy-done((f32[4096,64]{1,0:T(8,128)S(1)}, f32[4096,64]{1,0:T(8,128)}, u32[]{:S(2)}) %copy-start.2) | copy-done | bytes 1048600
  39.2 9.3 %face_exchange.3.recv_ref = f32[4,4,64,128]{3,2,1,0:T(8,128)S(1)} custom-call(s32[32]{0:T(128)S(1)} %reshape.46.faces_ref, f32[64,64,64]{2,1,0:T(8,128)S(1)} %bitcast.34), custom_call_target="tpu_custom_call" | custom-call | tf_op jit(solution)/shard_map/face_exchange/pallas_call | solution.py:104
  48.6 12.0 %operator_second.1 = (f32[4096,64]{1,0:T(8,128)S(1)}, f32[192,128]{1,0:T(8,128)S(1)}) custom-call(s32[384]{0:T(512)S(1)} %reshape.44.neigh_ref, bf16[64,128,448]{2,1,0:T(8,128)(2,1)} %get-tuple-element.9.left_ref, f32[64,64,64]{2,1,0:T(8,128)S(1)} %bitcast.35, f32[4,4,64,128]{3,2,1,0:T(8,128)S(1)} %face_exchange.3.recv_ref, f32[4096,64]{1,0:T(8,128)} %bitcast.33, ...), custom_call_target="tpu_custom_call" | custom-call | tf_op jit(solution)/shard_map/operator_second/pallas_call | solution.py:240
  60.6 1.3 %copy-done.5 = f32[4096,64]{1,0:T(8,128)} copy-done((f32[4096,64]{1,0:T(8,128)}, f32[4096,64]{1,0:T(8,128)S(1)}, u32[]{:S(2)}) %copy-start.5) | copy-done | bytes 1048600
  62.0 18.6 %gram_sum.1.gram_ref = f32[192,128]{1,0:T(8,128)S(1)} custom-call(f32[192,128]{1,0:T(8,128)S(1)} %get-tuple-element.11.part_ref), custom_call_target="tpu_custom_call" | custom-call | tf_op jit(solution)/shard_map/gram_sum/pallas_call | solution.py:321
  80.6 0.6 copy-done.9
  81.3 14.4 %small_solves.1.mix_ref = f32[128,64]{1,0:T(8,128)} custom-call(f32[192,128]{1,0:T(8,128)} %copy-done.9), custom_call_target="tpu_custom_call" | custom-call | tf_op jit(solution)/shard_map/small_solves/pallas_call | solution.py:382
  95.7 1.6 %copy-done.6 = f32[4096,64]{1,0:T(8,128)S(1)} copy-done((f32[4096,64]{1,0:T(8,128)S(1)}, f32[4096,64]{1,0:T(8,128)}, u32[]{:S(2)}) %copy-start.6) | copy-done | bytes 1048600
  97.3 0.8 copy-done.7
  98.1 9.0 %final_fields.1 = (f32[64,4096]{1,0:T(8,128)}, f32[64,4096]{1,0:T(8,128)}) custom-call(f32[128,64]{1,0:T(8,128)S(1)} %copy-done.7, f32[64,4096]{1,0:T(8,128)S(1)} %copy-done.4, f32[4096,64]{1,0:T(8,128)S(1)} %copy-done.3, f32[4096,64]{1,0:T(8,128)S(1)} %copy-done.6), custom_call_target="tpu_custom_call" | custom-call | tf_op jit(solution)/shard_map/final_fields/pallas_call | solution.py:406
  107.1 0.4 fusion.4
  107.5 0.8 reshape.51
  (27 shorter events, 0.1 us)
Async XLA Ops:
  0.6 1.9 %copy-start.13 = (s32[4,8]{1,0:T(4,128)S(1)}, s32[4,8]{1,0:T(4,128)}, u32[]{:S(2)}) copy-start(s32[4,8]{1,0:T(4,128)} %param.9) | copy-start | bytes 388
  0.6 2.0 %copy-start.12 = (s32[64,6]{0,1:T(8,128)S(1)}, s32[64,6]{0,1:T(8,128)}, u32[]{:S(2)}) copy-start(s32[64,6]{0,1:T(8,128)} %param.8) | copy-start | bytes 4612
  0.7 2.2 %copy-start.11 = (s32[512,1]{0,1:T(1,128)S(1)}, s32[512,1]{0,1:T(1,128)}, u32[]{:S(2)}) copy-start(s32[512,1]{0,1:T(1,128)} %param.10) | copy-start | bytes 6148
  2.5 25.5 %copy-start = (f32[64,4096]{0,1:T(8,128)}, f32[64,4096]{0,1:T(8,128)S(1)}, u32[]{:S(2)}) copy-start(f32[64,4096]{0,1:T(8,128)S(1)} %copy.11) | copy-start | bytes 3145732
  16.8 11.2 %copy-start.10 = (s32[512]{0:T(512)S(1)}, s32[512]{0:T(512)}, u32[]{:S(2)}) copy-start(s32[512]{0:T(512)} %node_ref.1) | copy-start | bytes 6148
  28.0 6.2 %copy-start.1 = (f32[4096,64]{1,0:T(8,128)}, f32[4096,64]{1,0:T(8,128)S(1)}, u32[]{:S(2)}) copy-start(f32[4096,64]{1,0:T(8,128)S(1)} %get-tuple-element.10.near_ref.image_ref) | copy-start | bytes 3145732
  34.2 72.9 %all-to-all-start = ((f32[4,128,128]{2,1,0:T(8,128)}), f32[4,128,128]{2,1,0:T(8,128)S(1)}, u32[]{:S(2)}, u32[]{:S(2)}) async-start(f32[4,128,128]{2,1,0:T(8,128)} %bitcast.8), calls=%async_computation | async-start | bytes 524288 | tf_op jit(solution)/shard_map/all_to_all | solution.py:457
  37.6 1.6 %copy-start.2 = (f32[4096,64]{1,0:T(8,128)S(1)}, f32[4096,64]{1,0:T(8,128)}, u32[]{:S(2)}) copy-start(f32[4096,64]{1,0:T(8,128)} %copy-done.1) | copy-start | bytes 3145732
  48.6 47.1 %copy-start.3 = (f32[4096,64]{1,0:T(8,128)S(1)}, f32[4096,64]{1,0:T(8,128)}, u32[]{:S(2)}) copy-start(f32[4096,64]{1,0:T(8,128)} %copy-done.1) | copy-start | bytes 3145732
  48.6 47.1 %copy-start.4 = (f32[64,4096]{1,0:T(8,128)S(1)}, f32[64,4096]{1,0:T(8,128)}, u32[]{:S(2)}) copy-start(f32[64,4096]{1,0:T(8,128)} %base_ref.1) | copy-start | bytes 3145732
  60.6 1.3 %copy-start.5 = (f32[4096,64]{1,0:T(8,128)}, f32[4096,64]{1,0:T(8,128)S(1)}, u32[]{:S(2)}) copy-start(f32[4096,64]{1,0:T(8,128)S(1)} %get-tuple-element.12.twice_ref) | copy-start | bytes 3145732
  80.6 0.6 copy-start.9
  95.7 1.6 %copy-start.6 = (f32[4096,64]{1,0:T(8,128)S(1)}, f32[4096,64]{1,0:T(8,128)}, u32[]{:S(2)}) copy-start(f32[4096,64]{1,0:T(8,128)} %copy-done.5) | copy-start | bytes 3145732
  97.3 0.8 copy-start.7
  98.1 9.0 %copy-start.8 = (f32[128,64]{1,0:T(8,128)S(1)}, f32[128,64]{1,0:T(8,128)}, u32[]{:S(2)}) copy-start(f32[128,64]{1,0:T(8,128)} %small_solves.1.mix_ref) | copy-start | bytes 98308
